TPU v7x, 256 devices: a whole 4x4x8 slice. The times are simulated.
256 devices in a mesh: hour: 32 (over z_hi, x, y), site: 8 (over z_lo, core).
Axes of the slice: x: 4, y: 4, z: 8 (z_hi: 2, z_lo: 4; z = z_hi * 4 + z_lo), core: 2. Of those that a mesh axis runs over, the one named last changes fastest.
Arguments:
- fields: bfloat16 [5120, 20480], P('hour', 'site'), may hold values from -6 to 6
- time_basis: bfloat16 [5120, 1536], P('hour'), may hold values from -0.15625 to 0.15625
- features: bfloat16 [20480, 2048], P('site'), may hold values from -0.1875 to 0.1875
- time_spectrum: float32 [1536], replicated, may hold values from 0.05 to 5
- feature_spectrum: float32 [2048], replicated, may hold values from 0.05 to 5
Outputs:
- solved: bfloat16 [5120, 20480], P('hour', 'site')
All inputs are finite; a program needn't handle non-finite values.
Results may differ from a plain program's by a relative error of at most 0.009.
Values may be sent and summed in bfloat16 or wider, within the bound.
A program may use at most 64 MiB of HBM per device.

v0:
```python
import jax
import jax.numpy as jnp
from jax import lax
from jax.sharding import PartitionSpec as P

noise_var = 0.1


def per_device(fields, time_basis, features, time_spectrum, feature_spectrum):
    feat_share = features.shape[1] // lax.axis_size("site")
    columns = features
    projected = lax.psum_scatter(
        lax.dot_general(
            columns, fields, (((0,), (1,)), ((), ())), preferred_element_type=jnp.float32
        ),
        "site",
        scatter_dimension=0,
        tiled=True,
    ).astype(jnp.bfloat16)
    feat_values = lax.dynamic_slice_in_dim(
        feature_spectrum, lax.axis_index("site") * feat_share, feat_share, 0
    )
    columns = time_basis
    coefficients = lax.psum(
        lax.dot_general(
            columns, projected, (((0,), (1,)), ((), ())), preferred_element_type=jnp.float32
        ),
        "hour",
    )
    denominator = time_spectrum[:, None] + feat_values[None, :] + noise_var
    scaled = (coefficients / denominator).astype(jnp.bfloat16)
    mixed = jnp.dot(time_basis, scaled, preferred_element_type=jnp.float32)
    mixed = mixed.astype(jnp.bfloat16)
    columns = features
    solved = lax.dot_general(
        lax.all_gather(mixed, "site", axis=1, tiled=True),
        columns,
        (((1,), (1,)), ((), ())),
        preferred_element_type=jnp.float32,
    )
    return solved.astype(jnp.bfloat16)


def solution(mesh):
    in_specs = (P("hour", "site"), P("hour", None), P("site", None), P(), P())
    out_specs = P("hour", "site")
    return jax.shard_map(
        per_device, mesh=mesh, in_specs=in_specs, out_specs=out_specs, check_vma=False
    )
```

profile of v0, /device:TPU:1, one launch (start us, length us, event | category | flops | bytes accessed | tf_op | source)
XLA Modules:
  0.0 528.5 jit_solution(10092935918751341472)
XLA Ops:
  6.5 0.0 copy-start
  6.5 0.0 reduce-scatter.2.cloned.1.call-start
  6.5 1.1 copy-done
  7.7 8.4 %fusion.3 = f32[2048,160]{1,0:T(8,128)} fusion(bf16[2560,2048]{1,0:T(8,128)(2,1)} %param.7, bf16[160,2560]{1,0:T(8,128)(2,1)S(1)} %copy-done), kind=kOutput, calls=%fused_computation.7 | convolution fusion | flops 1677721600 | bytes 12615680 | tf_op jit(solution)/shard_map/dot_general | solution.py:13
  16.1 0.0 copy-start.1
  16.1 0.0 reduce-scatter.2.cloned.1.call-update
  16.1 0.0 copy-start.2
  16.1 0.0 all-reduce.2.cloned.1.call-start
  16.2 42.3 %reduce-scatter.2.cloned.1.call-done = f32[256,160]{1,0:T(8,128)} async-done(((f32[2048,160]{1,0:T(8,128)}), f32[256,160]{1,0:T(8,128)}) %reduce-scatter.2.cloned.1.call-update) | async-done | bytes 163856 | tf_op jit(solution)/shard_map/reduce_scatter | solution.py:12
  58.4 0.0 copy-done.1
  58.4 2.5 convolution_bitcast_fusion
  60.9 0.0 all-reduce.2.cloned.1.call-update
  60.9 0.8 dynamic_slice.3
  61.7 410.5 %all-reduce.2.cloned.1.call-done = f32[1536,256]{0,1:T(8,128)} async-done(((f32[1536,256]{0,1:T(8,128)}), f32[1536,256]{0,1:T(8,128)}) %all-reduce.2.cloned.1.call-update) | async-done | bytes 1572880 | tf_op jit(solution)/shard_map/psum | solution.py:24
  472.1 0.0 copy-done.2
  472.2 1.8 fusion
  474.0 38.9 %all_gather.3 = bf16[160,2048]{0,1:T(8,128)(2,1)S(1)} all-gather(bf16[160,256]{0,1:T(8,128)(2,1)S(1)} %fusion), channel_id=1, replica_groups=mesh['hour'=32,'site'=8] {'site'}, dimensions={1}, use_global_device_ids=true | all-gather | bytes 737280 | tf_op jit(solution)/shard_map/all_gather | solution.py:36
  512.9 8.7 %convolution_convert_fusion = bf16[160,2560]{1,0:T(8,128)(2,1)} fusion(bf16[160,2048]{0,1:T(8,128)(2,1)S(1)} %all_gather.3, bf16[2560,2048]{1,0:T(8,128)(2,1)} %param.7), kind=kOutput, calls=%fused_computation | convolution fusion | flops 1678131200 | bytes 11960320 | tf_op jit(solution)/shard_map/dot_general | solution.py:35
Async XLA Ops:
  6.5 1.1 copy-start
  6.5 51.9 %reduce-scatter.2.cloned.1.call-start = ((), (), s32[]{:S(2)}) async-start(), calls=%async_computation.1 | async-start | bytes 2359296 | tf_op jit(solution)/shard_map/reduce_scatter | solution.py:12
  16.1 42.4 %copy-start.1 = (bf16[160,1536]{1,0:T(8,128)(2,1)S(1)}, bf16[160,1536]{1,0:T(8,128)(2,1)}, u32[]{:S(2)}) copy-start(bf16[160,1536]{1,0:T(8,128)(2,1)} %param.6) | copy-start | bytes 1474564
  16.1 456.1 %copy-start.2 = (f32[1536]{0:T(1024)S(1)}, f32[1536]{0:T(1024)}, u32[]{:S(2)}) copy-start(f32[1536]{0:T(1024)} %param.8) | copy-start | bytes 18436
  16.1 456.0 %all-reduce.2.cloned.1.call-start = ((), (), s32[]{:S(2)}) async-start(), calls=%async_computation.2 | async-start | bytes 3145728 | tf_op jit(solution)/shard_map/psum | solution.py:24
Sparse Core Ops, SparseCore 0:
  16.2 42.1 reduce-scatter.1
  61.0 411.0 all-reduce.1
where the time goes:
time: 529 us; the launch traced here: 528 us
  waiting for transfers between devices  453 us (86%)
  blocking collectives  38.9 us (7%)
  matrix products  21.4 us (4%)
  between operations  13.4 us (3%)
    psum x1, waiting for transfers between devices, per_device(): lax.psum(lax.dot_general(columns, projected, (((0,), (1,)), ((), ())), pr...  410 us
    reduce_scatter x1, waiting for transfers between devices, per_device(): lax.psum_scatter(lax.dot_general(columns, fields, (((0,), (1,)), ((), ())...  42.3 us
    all_gather x1, blocking collectives, per_device(): lax.all_gather(mixed, 'site', axis=1, tiled=True)  38.9 us
  transfers between devices with their start and end apart: 2, of which 2 were waited for; matrix products, arithmetic and copies ran while one was open for 0% of the time, Pallas kernels for 0%

commit v1 on v0

v1 whole, which is shorter than its diff:
```python
import jax
import jax.numpy as jnp
from jax import lax
from jax.experimental import pallas as pl
from jax.experimental.pallas import tpu as pltpu
from jax.sharding import PartitionSpec as P

noise_var = 0.1

RING = 8
PLANE = 16
FAR_FIRST = (4, 3, 5, 2, 6, 1, 7, 0)
NEAR_FIRST = (0, 1, 7, 2, 6, 3, 5, 4)
PLANE_FAR_FIRST = (10, 6, 14, 9, 11, 2, 8, 5, 7, 13, 15, 1, 3, 4, 12)
f32 = jnp.float32
bf16 = jnp.bfloat16


def kernel(fields, basis, features, ts_ref, fs_ref, out,
           feats, fbuf, t2, tt, cx_own, cx_send, cx_recv, zs_send, zs_recv,
           c_send, c_recv, s_own, s_all, m_send, m_all, acc, tcol,
           load_sem, feat_sem, t_send_sem, t_recv_sem, cx_ssem, cx_rsem, zs_ssem, zs_rsem,
           c_ssem, c_rsem, s_ssem, s_rsem, m_ssem, m_rsem, f_ssem, f_rsem):
    hour, site = lax.axis_index("hour"), lax.axis_index("site")
    zh, x, y = hour // 16, (hour // 4) % 4, hour % 4
    zl, core = site // 2, site % 2
    z = zh * 4 + zl
    rows = fields.shape[0]
    part = c_send.shape[0] // PLANE

    def at(z_, x_, y_, c_):
        return (((z_ // 4) * 4 + x_) * 4 + y_, (z_ % 4) * 2 + c_)

    def ring(d):
        return at((z + d) % RING, x, y, core)

    def plane(q):
        return at(z, (x + q // 4) % 4, (y + q % 4) % 4, core)

    sibling = at(z, x, y, 1 - core)

    def send(src, dst, ssem, rsem, device):
        copy = pltpu.make_async_remote_copy(
            src_ref=src, dst_ref=dst, send_sem=ssem, recv_sem=rsem,
            device_id=device, device_id_type=pl.DeviceIdType.MESH)
        copy.start()
        return copy

    barrier = pltpu.get_barrier_semaphore()
    for d in range(1, RING):
        pl.semaphore_signal(barrier, inc=1, device_id=ring(d), device_id_type=pl.DeviceIdType.MESH)
    for q in range(1, PLANE):
        pl.semaphore_signal(barrier, inc=1, device_id=plane(q), device_id_type=pl.DeviceIdType.MESH)
    pl.semaphore_signal(barrier, inc=1, device_id=sibling, device_id_type=pl.DeviceIdType.MESH)

    load_f = pltpu.make_async_copy(fields, fbuf, load_sem.at[0])
    load_f.start()
    own_t = pl.ds(pl.multiple_of(zh * rows, rows), rows)
    load_t = pltpu.make_async_copy(basis, t2.at[own_t], load_sem.at[1])
    loads = {}
    for i, d in enumerate(FAR_FIRST):
        col = pl.multiple_of(((z + d) % RING) * 256, 256)
        loads[d] = pltpu.make_async_copy(features.at[:, pl.ds(col, 256)], feats.at[d], feat_sem.at[d])
        loads[d].start()
        if i == 0:
            load_t.start()

    tcol[...] = jnp.broadcast_to(ts_ref[...], (128, ts_ref.shape[1])).T

    load_f.wait()
    load_t.wait()
    pl.semaphore_wait(barrier, RING - 1 + PLANE - 1 + 1)

    half = rows // 2
    mine_t = pl.ds(pl.multiple_of(zh * rows + core * half, half), half)
    near = (zl == 0) | (zl == 3)
    edge = jnp.where(zl == 0, -1, 1)
    edge_dev = at((z + edge + RING) % RING, x, y, core)
    inner_dev = at((z - edge + RING) % RING, x, y, core)
    other_t = pl.ds(pl.multiple_of((1 - zh) * rows + core * half, half), half)
    other_t2 = pl.ds(pl.multiple_of((1 - zh) * rows + (1 - core) * half, half), half)

    t_out = pltpu.make_async_remote_copy(
        src_ref=t2.at[mine_t], dst_ref=t2.at[mine_t], send_sem=t_send_sem.at[0], recv_sem=t_recv_sem.at[0],
        device_id=edge_dev, device_id_type=pl.DeviceIdType.MESH)
    t_in = pltpu.make_async_remote_copy(
        src_ref=t2.at[other_t], dst_ref=t2.at[other_t], send_sem=t_send_sem.at[1], recv_sem=t_recv_sem.at[0],
        device_id=inner_dev, device_id_type=pl.DeviceIdType.MESH)
    t_sib = pltpu.make_async_remote_copy(
        src_ref=t2.at[other_t], dst_ref=t2.at[other_t], send_sem=t_send_sem.at[2], recv_sem=t_recv_sem.at[1],
        device_id=sibling, device_id_type=pl.DeviceIdType.MESH)

    @pl.when(near)
    def _():
        t_out.start()

    cx, zs = {}, {}

    def mm1(d):
        loads[d].wait()
        block = jnp.dot(fbuf[...], feats[d], preferred_element_type=f32)
        low, high = block[:, :128], block[:, 128:]
        first = core == 0
        cx_own[d] = jnp.where(first, low, high)
        cx_send[d] = jnp.where(first, high, low).astype(bf16)
        cx[d] = send(cx_send.at[d], cx_recv.at[d], cx_ssem.at[d], cx_rsem.at[d], sibling)

    def pass_on(d):
        cx[d].wait_recv()
        total = (cx_own[d] + cx_recv[d].astype(f32)).astype(bf16)
        if d == 0:
            zs_recv[z] = total
        else:
            zs_send[d] = total
            zs[d] = send(zs_send.at[d], zs_recv.at[z], zs_ssem.at[d], zs_rsem.at[d], ring(d))

    SKEW = 2
    for i in range(RING + SKEW):
        if i < RING:
            mm1(FAR_FIRST[i])
        if i >= SKEW:
            pass_on(FAR_FIRST[i - SKEW])

    t_out.wait_recv()

    @pl.when(near)
    def _():
        t_in.start()

    t_sib.start()
    t_sib.wait_recv()
    tt[...] = t2[...].T

    for d in range(1, RING):
        zs[d].wait_recv()
    sum_a = (zs_recv[0].astype(f32) + zs_recv[1].astype(f32)) + (zs_recv[2].astype(f32) + zs_recv[3].astype(f32))
    sum_b = (zs_recv[4].astype(f32) + zs_recv[5].astype(f32)) + (zs_recv[6].astype(f32) + zs_recv[7].astype(f32))
    projected = jnp.concatenate([sum_a.astype(bf16), sum_b.astype(bf16)], axis=0)

    c_send[...] = jnp.dot(tt[...], projected, preferred_element_type=f32).astype(bf16)
    cs = {}
    for q in PLANE_FAR_FIRST:
        target = ((x + q // 4) % 4) * 4 + (y + q % 4) % 4
        src = c_send.at[pl.ds(pl.multiple_of(target * part, part), part)]
        cs[q] = send(src, c_recv.at[q], c_ssem.at[q], c_rsem.at[q], plane(q))
    own_r = pl.ds(pl.multiple_of((x * 4 + y) * part, part), part)
    total = c_send[own_r].astype(f32)
    col = pl.multiple_of(z * 256 + core * 128, 128)
    denom = tcol[own_r] + fs_ref[:, pl.ds(col, 128)] + noise_var
    for q in reversed(PLANE_FAR_FIRST):
        cs[q].wait_recv()
        total = total + c_recv[q].astype(f32)
    scaled = (total / denom).astype(bf16)
    s_own[...] = scaled
    s_all[own_r] = scaled
    ss = {}
    for q in PLANE_FAR_FIRST:
        ss[q] = send(s_own, s_all.at[own_r], s_ssem.at[q], s_rsem.at[q], plane(q))
    for q in reversed(PLANE_FAR_FIRST):
        ss[q].wait_recv()

    m_send[...] = jnp.dot(t2[...], s_all[...], preferred_element_type=f32).astype(bf16)
    ms = {}
    for d in FAR_FIRST[:-1]:
        dest = (z + d) % RING
        src = m_send.at[pl.ds(pl.multiple_of((dest // 4) * rows, rows), rows)]
        ms[d] = send(src, m_all.at[(RING - d) % RING, core], m_ssem.at[d], m_rsem.at[d], ring(d))
    m_all[0, core] = m_send[own_t]
    fw = {}

    def forward(d):
        if d:
            ms[RING - d].wait_recv()
        fw[d] = send(m_all.at[d, core], m_all.at[d, core], f_ssem.at[d], f_rsem.at[d], sibling)

    def mm4(d):
        fw[d].wait_recv()
        block = jnp.concatenate([m_all[d, 0], m_all[d, 1]], axis=1)
        add = lax.dot_general(block, feats[d], (((1,), (1,)), ((), ())), preferred_element_type=f32)
        if d == NEAR_FIRST[0]:
            acc[...] = add
        elif d == NEAR_FIRST[-1]:
            out[...] = (acc[...] + add).astype(out.dtype)
        else:
            acc[...] += add

    for i in range(RING + 1):
        if i < RING:
            forward(NEAR_FIRST[i])
        if i >= 1:
            mm4(NEAR_FIRST[i - 1])

    @pl.when(near)
    def _():
        t_out.wait_send()
        t_in.wait_send()

    t_sib.wait_send()
    for copies in (cx, zs, cs, ss, ms, fw):
        for copy in copies.values():
            copy.wait_send()


def per_device(fields, basis, features, time_spectrum, feature_spectrum):
    rows, sites = fields.shape
    n_basis = basis.shape[1]
    part = n_basis // PLANE
    any_space = pl.BlockSpec(memory_space=pl.ANY)
    vmem = pl.BlockSpec(memory_space=pltpu.VMEM)
    dma = pltpu.SemaphoreType.DMA
    return pl.pallas_call(
        kernel,
        out_shape=jax.ShapeDtypeStruct((rows, sites), bf16),
        in_specs=[any_space, any_space, any_space, vmem, vmem],
        out_specs=vmem,
        scratch_shapes=[
            pltpu.VMEM((RING, sites, 256), bf16),
            pltpu.VMEM((rows, sites), bf16),
            pltpu.VMEM((2 * rows, n_basis), bf16),
            pltpu.VMEM((n_basis, 2 * rows), bf16),
            pltpu.VMEM((RING, rows, 128), f32),
            pltpu.VMEM((RING, rows, 128), bf16),
            pltpu.VMEM((RING, rows, 128), bf16),
            pltpu.VMEM((RING, rows, 128), bf16),
            pltpu.VMEM((RING, rows, 128), bf16),
            pltpu.VMEM((n_basis, 128), bf16),
            pltpu.VMEM((PLANE, part, 128), bf16),
            pltpu.VMEM((part, 128), bf16),
            pltpu.VMEM((n_basis, 128), bf16),
            pltpu.VMEM((2 * rows, 128), bf16),
            pltpu.VMEM((RING, 2, rows, 128), bf16),
            pltpu.VMEM((rows, sites), f32),
            pltpu.VMEM((n_basis, 128), f32),
            dma((2,)), dma((RING,)), dma((3,)), dma((2,)),
            dma((RING,)), dma((RING,)), dma((RING,)), dma((RING,)),
            dma((PLANE,)), dma((PLANE,)), dma((PLANE,)), dma((PLANE,)),
            dma((RING,)), dma((RING,)), dma((RING,)), dma((RING,)),
        ],
        compiler_params=pltpu.CompilerParams(
            collective_id=0, has_side_effects=True, vmem_limit_bytes=48 * 2**20),
        cost_estimate=pl.CostEstimate(flops=3_600_000_000, bytes_accessed=13_000_000, transcendentals=0),
        name="solve",
    )(fields, basis, features, time_spectrum.reshape(1, -1), feature_spectrum.reshape(1, -1))


def solution(mesh):
    in_specs = (P("hour", "site"), P("hour", None), P("site", None), P(), P())
    out_specs = P("hour", "site")
    return jax.shard_map(
        per_device, mesh=mesh, in_specs=in_specs, out_specs=out_specs, check_vma=False
    )
```

time: 529 us -> 65.1 us (0.12)
  waiting for transfers between devices: 453 us -> 0 us
  Pallas kernels: 0 us -> 60.4 us
  blocking collectives: 38.9 us -> 0 us
  matrix products: 21.4 us -> 0 us
  between operations: 13.4 us -> 0.01 us
    psum x1 -> x0, waiting for transfers between devices: 410 us -> none  [per_device(): lax.psum(lax.dot_general(columns, projected, (((0,), (1,)), ((), ())), pr...]
    pallas_call x0 -> x1, Pallas kernels: none -> 60.4 us  [per_device(): pl.pallas_call(kernel, out_shape=jax.ShapeDtypeStruct((rows, sites), bf16...]
    reduce_scatter x1 -> x0, waiting for transfers between devices: 42.3 us -> none  [per_device(): lax.psum_scatter(lax.dot_general(columns, fields, (((0,), (1,)), ((), ())...]
    all_gather x1 -> x0, blocking collectives: 38.9 us -> none  [per_device(): lax.all_gather(mixed, 'site', axis=1, tiled=True)]
    dot_general x4 -> x0, matrix products: 21.4 us -> none  [the longest x1 8.69 us: per_device(): lax.dot_general(lax.all_gather(mixed, 'site', axis=1, tiled=True), column...]
  transfers between devices with their start and end apart: 2 -> 0, of which waited for: 2 -> 0; matrix products, arithmetic and copies ran while one was open for 0% -> 0% of each run, Pallas kernels for 0% -> 0%
where the time goes in v1:
time: 65.1 us; the launch traced here: 64.9 us
  Pallas kernels  60.4 us (93%)
  local copies, waits for them, and re-layouts  4.46 us (7%)
    pallas_call x1, Pallas kernels, per_device(): pl.pallas_call(kernel, out_shape=jax.ShapeDtypeStruct((rows, sites), bf16...  60.4 us
    unnamed x7, local copies, waits for them, and re-layouts  3.76 us

profile of v1, /device:TPU:1, one launch (start us, length us, event | category | flops | bytes accessed | tf_op | source)
XLA Modules:
  0.0 64.9 jit_solution(958014744898867428)
XLA Ops:
  0.0 0.7 %reshape.6.ts_ref = f32[1,1536]{1,0:T(1,128)S(1)} reshape(f32[1536]{0:T(1024)} %param.8) | data formatting | bytes 12288 | tf_op jit(solution)/shard_map/reshape | solution.py:243
  0.7 0.0 copy-start
  0.7 1.1 %copy-done = bf16[160,2560]{1,0:T(8,128)(2,1)S(1)} copy-done((bf16[160,2560]{1,0:T(8,128)(2,1)S(1)}, bf16[160,2560]{1,0:T(8,128)(2,1)}, u32[]{:S(2)}) %copy-start) | copy-done | bytes 819224
  1.8 0.0 copy-start.1
  1.8 1.0 %copy-done.1 = bf16[160,1536]{1,0:T(8,128)(2,1)S(1)} copy-done((bf16[160,1536]{1,0:T(8,128)(2,1)S(1)}, bf16[160,1536]{1,0:T(8,128)(2,1)}, u32[]{:S(2)}) %copy-start.1) | copy-done | bytes 491544
  2.9 0.0 copy-start.2
  2.9 0.7 %copy-done.2 = f32[2048]{0:T(1024)S(1)} copy-done((f32[2048]{0:T(1024)S(1)}, f32[2048]{0:T(1024)}, u32[]{:S(2)}) %copy-start.2) | copy-done | bytes 8216
  3.6 60.4 %solve.1 = bf16[160,2560]{1,0:T(8,128)(2,1)S(1)} custom-call(bf16[160,2560]{1,0:T(8,128)(2,1)S(1)} %copy-done, bf16[160,1536]{1,0:T(8,128)(2,1)S(1)} %copy-done.1, bf16[2560,2048]{1,0:T(8,128)(2,1)} %features.1, f32[1,1536]{1,0:T(1,128)S(1)} %reshape.6.ts_ref, f32[1,2048]{1,0:T(1,128)S(1)} %bitcast.1), custom_call_target="tpu_custom_call" | custom-call | flops 3600000000 | bytes 13000000 | tf_op jit(solution)/shard_map/solve/pallas_call | solution.py:211
  64.0 0.9 %copy.7 = bf16[160,2560]{1,0:T(8,128)(2,1)} copy(bf16[160,2560]{1,0:T(8,128)(2,1)S(1)} %solve.1) | data formatting | bytes 1638400
Async XLA Ops:
  0.7 1.1 %copy-start = (bf16[160,2560]{1,0:T(8,128)(2,1)S(1)}, bf16[160,2560]{1,0:T(8,128)(2,1)}, u32[]{:S(2)}) copy-start(bf16[160,2560]{1,0:T(8,128)(2,1)} %fields.1) | copy-start | bytes 2457604
  1.8 1.0 %copy-start.1 = (bf16[160,1536]{1,0:T(8,128)(2,1)S(1)}, bf16[160,1536]{1,0:T(8,128)(2,1)}, u32[]{:S(2)}) copy-start(bf16[160,1536]{1,0:T(8,128)(2,1)} %basis.1) | copy-start | bytes 1474564
  2.9 0.7 %copy-start.2 = (f32[2048]{0:T(1024)S(1)}, f32[2048]{0:T(1024)}, u32[]{:S(2)}) copy-start(f32[2048]{0:T(1024)} %param.9) | copy-start | bytes 24580

commit v2 on v0

v2 whole, which is shorter than its diff:
```python
import jax
import jax.numpy as jnp
from jax import lax
from jax.experimental import pallas as pl
from jax.experimental.pallas import tpu as pltpu
from jax.sharding import PartitionSpec as P

noise_var = 0.1

RING = 8
PAIRS = 4
PLANE = 16
CHUNKS = 2
LANES = 128
PAIR_ORDER = (2, 1, 3, 0)
PLANE_FAR_FIRST = (10, 6, 14, 9, 11, 2, 8, 5, 7, 13, 15, 1, 3, 4, 12)
f32 = jnp.float32
bf16 = jnp.bfloat16


def kernel(fields, basis, features, ts_hbm, fs_hbm, out,
           ts_ref, fs_ref, feats, featst, fbuf, t2, tt, tcol, acc,
           cx_own, cx_send, cx_recv, zs_send, zs_recv,
           c_send, c_recv, s_own, s_all, m_send, m_all,
           load_sem, feat_sem, t_ssem, t_rsem, u_ssem, u_rsem, cx_ssem, cx_rsem,
           zs_ssem, zs_rsem, c_ssem, c_rsem, s_ssem, s_rsem, m_ssem, m_rsem, f_ssem, f_rsem):
    hour, site = lax.axis_index("hour"), lax.axis_index("site")
    zh, x, y = hour // 16, (hour // 4) % 4, hour % 4
    zl, core = site // 2, site % 2
    z = zh * 4 + zl
    odd = z % 2
    rows = fields.shape[0]
    half = rows // 2
    n_basis = basis.shape[1]
    mid = n_basis // 2
    width = features.shape[1] // CHUNKS
    part = mid // PLANE
    left = lax.broadcasted_iota(jnp.int32, (1, LANES), 1) < LANES // 2

    def at(z_, x_, y_, c_):
        return (((z_ // 4) * 4 + x_) * 4 + y_, (z_ % 4) * 2 + c_)

    def ring(z_):
        return at(z_, x, y, core)

    def plane(q):
        return at(z, (x + q // 4) % 4, (y + q % 4) % 4, core)

    def in_pair(m, e):
        return ((z // 2 + m) % PAIRS) * 2 + e

    sibling = at(z, x, y, 1 - core)

    def remote(src, dst, ssem, rsem, device):
        return pltpu.make_async_remote_copy(
            src_ref=src, dst_ref=dst, send_sem=ssem, recv_sem=rsem,
            device_id=device, device_id_type=pl.DeviceIdType.MESH)

    def send(*args):
        copy = remote(*args)
        copy.start()
        return copy

    def swap(v):
        return pltpu.roll(v, LANES // 2, axis=1)

    barrier = pltpu.get_barrier_semaphore()
    for d in range(1, RING):
        pl.semaphore_signal(barrier, inc=1, device_id=ring((z + d) % RING), device_id_type=pl.DeviceIdType.MESH)
    for q in range(1, PLANE):
        pl.semaphore_signal(barrier, inc=1, device_id=plane(q), device_id_type=pl.DeviceIdType.MESH)
    pl.semaphore_signal(barrier, inc=1, device_id=sibling, device_id_type=pl.DeviceIdType.MESH)

    load_t = pltpu.make_async_copy(basis, t2.at[0], load_sem.at[1])
    load_t.start()
    load_f = pltpu.make_async_copy(fields, fbuf, load_sem.at[0])
    load_f.start()
    load_ts = pltpu.make_async_copy(ts_hbm, ts_ref, load_sem.at[2])
    load_ts.start()
    load_fs = pltpu.make_async_copy(fs_hbm, fs_ref, load_sem.at[3])
    load_fs.start()
    loads = {}
    for k in range(CHUNKS):
        for m in PAIR_ORDER:
            col = pl.multiple_of(k * width + ((z // 2 + m) % PAIRS) * 256, 256)
            loads[k, m] = pltpu.make_async_copy(
                features.at[:, pl.ds(col, 256)], feats.at[k, m], feat_sem.at[k, m])
            loads[k, m].start()

    load_ts.wait()
    load_fs.wait()
    tcol[...] = jnp.broadcast_to(ts_ref[...][None, :], (LANES, n_basis)).T
    load_t.wait()
    pl.semaphore_wait(barrier, RING - 1 + PLANE - 1 + 1)

    near = (zl == 0) | (zl == 3)
    edge = jnp.where(zl == 0, RING - 1, 1)
    edge_dev = ring((z + edge) % RING)
    inner_dev = ring((z + RING - edge) % RING)
    my_half = pl.ds(pl.multiple_of(core * half, half), half)
    t_out, t_on, t_sib = [], [], []
    for i in range(2):
        piece = pl.ds(i * mid, mid)
        mine, other = t2.at[0, my_half, piece], t2.at[1, my_half, piece]
        t_out.append(remote(mine, other, t_ssem.at[0, i], t_rsem.at[i], edge_dev))
        t_on.append(remote(other, other, t_ssem.at[1, i], t_rsem.at[i], inner_dev))
        t_sib.append(remote(other, other, u_ssem.at[i], u_rsem.at[i], sibling))

    @pl.when(near)
    def _():
        t_out[0].start()
        t_out[1].start()

    load_f.wait()
    cx, zs = {}, {}

    def mm1(k, m):
        loads[k, m].wait()
        block = jnp.dot(fbuf[...], feats[k, m], preferred_element_type=f32)
        for e in range(2):
            top, low = block[:half, e * LANES:(e + 1) * LANES], block[half:, e * LANES:(e + 1) * LANES]
            first = jnp.where(left, top, swap(low))
            second = jnp.where(left, swap(top), low)
            cx_own[k, m, e] = jnp.where(core == 0, first, second)
            cx_send[k, m, e] = jnp.where(core == 0, second, first)
        cx[k, m] = send(cx_send.at[k, m], cx_recv.at[k, m], cx_ssem.at[k, m], cx_rsem.at[k, m], sibling)

    def pass_on(k, m):
        cx[k, m].wait_recv()
        if m:
            for e in range(2):
                zs_send[k, m, e] = (cx_own[k, m, e] + cx_recv[k, m, e]).astype(bf16)
                zs[k, m, e] = send(zs_send.at[k, m, e], zs_recv.at[k, z], zs_ssem.at[k, m, e],
                                   zs_rsem.at[k, PAIRS - m, odd], ring(in_pair(m, e)))
        else:
            zs_send[k, 0, 0] = (cx_own[k, 0, 1 - odd] + cx_recv[k, 0, 1 - odd]).astype(bf16)
            zs[k, 0, 0] = send(zs_send.at[k, 0, 0], zs_recv.at[k, z], zs_ssem.at[k, 0, 0],
                               zs_rsem.at[k, 0, odd], ring(in_pair(0, 1 - odd)))
            zs_recv[k, z] = (cx_own[k, 0, odd] + cx_recv[k, 0, odd]).astype(bf16)

    SKEW = 3
    blocks = [(k, m) for k in range(CHUNKS) for m in PAIR_ORDER]
    for i in range(len(blocks)):
        mm1(*blocks[i])
        if SKEW <= i < SKEW + PAIRS:
            pass_on(*blocks[i - SKEW])

    def t_arrived(i):
        t_out[i].wait_recv()
        t_sib[i].start()

    @pl.when(near)
    def _():
        for i in range(2):
            t_out[i].wait_recv()
            t_on[i].start()
            t_sib[i].start()

    tt[0] = t2[0].T
    for k in range(1, CHUNKS):
        for copy in [c for (kk, *_), c in zs.items() if kk == k - 1]:
            copy.wait_send()
        for m in PAIR_ORDER:
            pass_on(k, m)

    @pl.when(jnp.logical_not(near))
    def _():
        for i in range(2):
            t_out[i].wait_recv()
            t_sib[i].start()

    for i in range(2):
        t_sib[i].wait_recv()
    tt[1] = t2[1].T

    cs, ss, ms, fw = {}, {}, {}, {}

    def wait_ring(k, sem, src, dst):
        for m in range(PAIRS):
            for e in range(2):
                if m:
                    remote(src, dst, sem.at[k, m, e], sem.at[k, m, e], sibling).wait_recv()
        other = sem.at[k, 0, 1 - odd]
        remote(src, dst, other, other, sibling).wait_recv()

    def mm2(k):
        wait_ring(k, zs_rsem, zs_send.at[k, 0, 0], zs_recv.at[k, 0])
        total = None
        for g in range(2):
            base = (zh if g == 0 else 1 - zh) * 4
            packed = ((zs_recv[k, base].astype(f32) + zs_recv[k, base + 1].astype(f32))
                      + (zs_recv[k, base + 2].astype(f32) + zs_recv[k, base + 3].astype(f32)))
            swapped = swap(packed)
            low = jnp.concatenate([jnp.where(left, packed, 0), jnp.where(left, swapped, 0)], axis=0).astype(bf16)
            high = jnp.concatenate([jnp.where(left, 0, swapped), jnp.where(left, 0, packed)], axis=0).astype(bf16)
            add = (jnp.dot(tt[g, :mid], low, preferred_element_type=f32)
                   + jnp.dot(tt[g, mid:], high, preferred_element_type=f32))
            total = add if total is None else total + add
        c_send[k] = total.astype(bf16)
        for q in PLANE_FAR_FIRST:
            target = ((x + q // 4) % 4) * 4 + (y + q % 4) % 4
            src = c_send.at[k, pl.ds(pl.multiple_of(target * part, part), part)]
            cs[k, q] = send(src, c_recv.at[k, q], c_ssem.at[k, q], c_rsem.at[k, q], plane(q))

    mine_r = (x * 4 + y) * part
    own_r = pl.ds(pl.multiple_of(mine_r, part), part)
    own_r2 = pl.ds(pl.multiple_of(mid + mine_r, part), part)

    def scale(k):
        total = c_send[k, own_r].astype(f32)
        own_f = fs_ref[pl.ds(pl.multiple_of(k * width + z * LANES, LANES), LANES)][None, :]
        other_f = swap(jnp.broadcast_to(own_f, (8, LANES)))[:1]
        both = jnp.where(left == (core == 0), own_f, other_f)
        denom = jnp.where(left, tcol[own_r], tcol[own_r2]) + both + noise_var
        for q in reversed(PLANE_FAR_FIRST):
            cs[k, q].wait_recv()
            total = total + c_recv[k, q].astype(f32)
        scaled = (total / denom).astype(bf16)
        s_own[k] = scaled
        s_all[k, own_r] = scaled
        for q in PLANE_FAR_FIRST:
            ss[k, q] = send(s_own.at[k], s_all.at[k, own_r], s_ssem.at[k, q], s_rsem.at[k, q], plane(q))

    def mm3(k):
        for q in reversed(PLANE_FAR_FIRST):
            ss[k, q].wait_recv()
        for g in range(2):
            first = jnp.dot(t2[g, :, :mid], s_all[k], preferred_element_type=f32)
            second = jnp.dot(t2[g, :, mid:], s_all[k], preferred_element_type=f32)
            both = jnp.where(left, first, second)
            both = both + swap(both)
            m_send[k, g] = jnp.where(left, both[:half], both[half:]).astype(bf16)
        for m in PAIR_ORDER[:-1]:
            for e in range(2):
                dest = in_pair(m, e)
                ms[k, m, e] = send(m_send.at[k, (dest // 4 + zh) % 2], m_all.at[k, PAIRS - m, odd, core],
                                   m_ssem.at[k, m, e], m_rsem.at[k, PAIRS - m, odd], ring(dest))
        ms[k, 0, 0] = send(m_send.at[k, 0], m_all.at[k, 0, odd, core],
                           m_ssem.at[k, 0, 0], m_rsem.at[k, 0, odd], ring(in_pair(0, 1 - odd)))
        m_all[k, 0, odd, core] = m_send[k, 0]

    def forward(k, m, e, wait=True):
        slot = m_all.at[k, m, e, core]
        if wait:
            sem = m_rsem.at[k, m, e]
            remote(slot, slot, sem, sem, sibling).wait_recv()
        fw[k, m, e if isinstance(e, int) else wait] = send(slot, slot, f_ssem.at[k, m, e], f_rsem.at[k, m, e], sibling)

    def forward_all(k):
        forward(k, 0, odd, wait=False)
        forward(k, 0, 1 - odd)
        for m in (1, 3, 2):
            for e in range(2):
                forward(k, m, e)

    def mm4(k):
        total = None
        for m in (0, 1, 3, 2):
            sides = []
            for e in range(2):
                slot = m_all.at[k, m, e, core]
                remote(slot, slot, f_ssem.at[k, m, e], f_rsem.at[k, m, e], sibling).wait_recv()
                first, second = m_all[k, m, e, 0].astype(f32), m_all[k, m, e, 1].astype(f32)
                sides.append(jnp.concatenate([jnp.where(left, first, swap(second)),
                                              jnp.where(left, swap(first), second)], axis=0).astype(bf16))
            block = jnp.concatenate(sides, axis=1)
            add = jnp.dot(block, featst[k, m], preferred_element_type=f32)
            total = add if total is None else total + add
        if k == 0:
            acc[...] = total
        else:
            out[...] = (acc[...] + total).astype(out.dtype)

    def turn(k):
        for m in range(PAIRS):
            featst[k, m] = feats[k, m].T

    mm2(0)
    mm2(1)
    turn(0)
    scale(0)
    scale(1)
    turn(1)
    mm3(0)
    mm3(1)
    forward_all(0)
    mm4(0)
    forward_all(1)
    mm4(1)

    @pl.when(near)
    def _():
        for copy in t_out + t_on:
            copy.wait_send()

    for copy in t_sib:
        copy.wait_send()
    for key, copy in zs.items():
        if key[0] == CHUNKS - 1:
            copy.wait_send()
    for copies in (cx, cs, ss, ms, fw):
        for copy in copies.values():
            copy.wait_send()


def per_device(fields, basis, features, time_spectrum, feature_spectrum):
    rows, sites = fields.shape
    half = rows // 2
    n_basis = basis.shape[1]
    mid = n_basis // 2
    part = mid // PLANE
    any_space = pl.BlockSpec(memory_space=pl.ANY)
    dma = pltpu.SemaphoreType.DMA
    return pl.pallas_call(
        kernel,
        out_shape=jax.ShapeDtypeStruct((rows, sites), bf16),
        in_specs=[any_space] * 5,
        out_specs=pl.BlockSpec(memory_space=pltpu.VMEM),
        scratch_shapes=[
            pltpu.VMEM(time_spectrum.shape, f32),
            pltpu.VMEM(feature_spectrum.shape, f32),
            pltpu.VMEM((CHUNKS, PAIRS, sites, 256), bf16),
            pltpu.VMEM((CHUNKS, PAIRS, 256, sites), bf16),
            pltpu.VMEM((rows, sites), bf16),
            pltpu.VMEM((2, rows, n_basis), bf16),
            pltpu.VMEM((2, n_basis, rows), bf16),
            pltpu.VMEM((n_basis, LANES), f32),
            pltpu.VMEM((rows, sites), f32),
            pltpu.VMEM((CHUNKS, PAIRS, 2, half, LANES), f32),
            pltpu.VMEM((CHUNKS, PAIRS, 2, half, LANES), f32),
            pltpu.VMEM((CHUNKS, PAIRS, 2, half, LANES), f32),
            pltpu.VMEM((CHUNKS, PAIRS, 2, half, LANES), bf16),
            pltpu.VMEM((CHUNKS, RING, half, LANES), bf16),
            pltpu.VMEM((CHUNKS, mid, LANES), bf16),
            pltpu.VMEM((CHUNKS, PLANE, part, LANES), bf16),
            pltpu.VMEM((CHUNKS, part, LANES), bf16),
            pltpu.VMEM((CHUNKS, mid, LANES), bf16),
            pltpu.VMEM((CHUNKS, 2, half, LANES), bf16),
            pltpu.VMEM((CHUNKS, PAIRS, 2, 2, half, LANES), bf16),
            dma((4,)), dma((CHUNKS, PAIRS)),
            dma((2, 2)), dma((2,)), dma((2,)), dma((2,)),
            dma((CHUNKS, PAIRS)), dma((CHUNKS, PAIRS)),
            dma((CHUNKS, PAIRS, 2)), dma((CHUNKS, PAIRS, 2)),
            dma((CHUNKS, PLANE)), dma((CHUNKS, PLANE)),
            dma((CHUNKS, PLANE)), dma((CHUNKS, PLANE)),
            dma((CHUNKS, PAIRS, 2)), dma((CHUNKS, PAIRS, 2)),
            dma((CHUNKS, PAIRS, 2)), dma((CHUNKS, PAIRS, 2)),
        ],
        compiler_params=pltpu.CompilerParams(
            collective_id=0, has_side_effects=True, vmem_limit_bytes=60 * 2**20),
        cost_estimate=pl.CostEstimate(flops=3_600_000_000, bytes_accessed=13_000_000, transcendentals=0),
        name="solve",
    )(fields, basis, features, time_spectrum, feature_spectrum)


def solution(mesh):
    in_specs = (P("hour", "site"), P("hour", None), P("site", None), P(), P())
    out_specs = P("hour", "site")
    return jax.shard_map(
        per_device, mesh=mesh, in_specs=in_specs, out_specs=out_specs, check_vma=False
    )
```

time: 529 us -> 58.4 us (0.11)
  waiting for transfers between devices: 453 us -> 0 us
  Pallas kernels: 0 us -> 56.2 us
  blocking collectives: 38.9 us -> 0 us
  matrix products: 21.4 us -> 0 us
  between operations: 13.4 us -> 0.01 us
    psum x1 -> x0, waiting for transfers between devices: 410 us -> none  [per_device(): lax.psum(lax.dot_general(columns, projected, (((0,), (1,)), ((), ())), pr...]
    pallas_call x0 -> x1, Pallas kernels: none -> 56.2 us  [per_device(): pl.pallas_call(kernel, out_shape=jax.ShapeDtypeStruct((rows, sites), bf16...]
    reduce_scatter x1 -> x0, waiting for transfers between devices: 42.3 us -> none  [per_device(): lax.psum_scatter(lax.dot_general(columns, fields, (((0,), (1,)), ((), ())...]
    all_gather x1 -> x0, blocking collectives: 38.9 us -> none  [per_device(): lax.all_gather(mixed, 'site', axis=1, tiled=True)]
    dot_general x4 -> x0, matrix products: 21.4 us -> none  [the longest x1 8.69 us: per_device(): lax.dot_general(lax.all_gather(mixed, 'site', axis=1, tiled=True), column...]
  transfers between devices with their start and end apart: 2 -> 0, of which waited for: 2 -> 0; matrix products, arithmetic and copies ran while one was open for 0% -> 0% of each run, Pallas kernels for 0% -> 0%
where the time goes in v2:
time: 58.4 us; the launch traced here: 58.3 us
  Pallas kernels  56.2 us (96%)
  local copies, waits for them, and re-layouts  2.09 us (4%)
    pallas_call x1, Pallas kernels, per_device(): pl.pallas_call(kernel, out_shape=jax.ShapeDtypeStruct((rows, sites), bf16...  56.2 us
    unnamed x1, local copies, waits for them, and re-layouts  2.09 us

profile of v2, /device:TPU:1, one launch (start us, length us, event | category | flops | bytes accessed | tf_op | source)
XLA Modules:
  0.0 58.3 jit_solution(17585933202794751516)
XLA Ops:
  0.0 56.2 %solve.1 = bf16[160,2560]{1,0:T(8,128)(2,1)} custom-call(bf16[160,2560]{1,0:T(8,128)(2,1)} %fields.1, bf16[160,1536]{1,0:T(8,128)(2,1)} %basis.1, bf16[2560,2048]{1,0:T(8,128)(2,1)} %features.1, f32[1536]{0:T(1024)} %ts_hbm.1, f32[2048]{0:T(1024)} %fs_hbm.1), custom_call_target="tpu_custom_call" | custom-call | flops 3600000000 | bytes 13000000 | tf_op jit(solution)/shard_map/solve/pallas_call | solution.py:314
  56.2 2.1 %copy.7 = bf16[160,2560]{1,0:T(8,128)(2,1)} copy(bf16[160,2560]{1,0:T(8,128)(2,1)} %solve.1) | data formatting | bytes 1638400

commit v3 on v2

--- a/solution.py
+++ b/solution.py
@@ -1,3 +1,5 @@
+import functools
+
 import jax
 import jax.numpy as jnp
 from jax import lax
@@ -11,6 +13,8 @@
 PAIRS = 4
 PLANE = 16
 CHUNKS = 2
+PIECES = 4
+SKEW = 2
 LANES = 128
 PAIR_ORDER = (2, 1, 3, 0)
 PLANE_FAR_FIRST = (10, 6, 14, 9, 11, 2, 8, 5, 7, 13, 15, 1, 3, 4, 12)
@@ -19,16 +23,16 @@
 
 
 def kernel(fields, basis, features, ts_hbm, fs_hbm, out,
-           ts_ref, fs_ref, feats, featst, fbuf, t2, tt, tcol, acc,
+           ts_ref, fs_ref, feats, featst, fbuf, t2, tcol, acc,
            cx_own, cx_send, cx_recv, zs_send, zs_recv,
            c_send, c_recv, s_own, s_all, m_send, m_all,
            load_sem, feat_sem, t_ssem, t_rsem, u_ssem, u_rsem, cx_ssem, cx_rsem,
            zs_ssem, zs_rsem, c_ssem, c_rsem, s_ssem, s_rsem, m_ssem, m_rsem, f_ssem, f_rsem):
     hour, site = lax.axis_index("hour"), lax.axis_index("site")
-    zh, x, y = hour // 16, (hour // 4) % 4, hour % 4
-    zl, core = site // 2, site % 2
+    zh, x, y = hour >> 4, (hour >> 2) & 3, hour & 3
+    zl, core = site >> 1, site & 1
     z = zh * 4 + zl
-    odd = z % 2
+    odd = z & 1
     rows = fields.shape[0]
     half = rows // 2
     n_basis = basis.shape[1]
@@ -38,16 +42,16 @@
     left = lax.broadcasted_iota(jnp.int32, (1, LANES), 1) < LANES // 2
 
     def at(z_, x_, y_, c_):
-        return (((z_ // 4) * 4 + x_) * 4 + y_, (z_ % 4) * 2 + c_)
+        return ((z_ >> 2) * 16 + x_ * 4 + y_, (z_ & 3) * 2 + c_)
 
     def ring(z_):
         return at(z_, x, y, core)
 
     def plane(q):
-        return at(z, (x + q // 4) % 4, (y + q % 4) % 4, core)
+        return at(z, (x + q // 4) & 3, (y + q % 4) & 3, core)
 
     def in_pair(m, e):
-        return ((z // 2 + m) % PAIRS) * 2 + e
+        return (((z >> 1) + m) & 3) * 2 + e
 
     sibling = at(z, x, y, 1 - core)
 
@@ -64,15 +68,6 @@
     def swap(v):
         return pltpu.roll(v, LANES // 2, axis=1)
 
-    barrier = pltpu.get_barrier_semaphore()
-    for d in range(1, RING):
-        pl.semaphore_signal(barrier, inc=1, device_id=ring((z + d) % RING), device_id_type=pl.DeviceIdType.MESH)
-    for q in range(1, PLANE):
-        pl.semaphore_signal(barrier, inc=1, device_id=plane(q), device_id_type=pl.DeviceIdType.MESH)
-    pl.semaphore_signal(barrier, inc=1, device_id=sibling, device_id_type=pl.DeviceIdType.MESH)
-
-    load_t = pltpu.make_async_copy(basis, t2.at[0], load_sem.at[1])
-    load_t.start()
     load_f = pltpu.make_async_copy(fields, fbuf, load_sem.at[0])
     load_f.start()
     load_ts = pltpu.make_async_copy(ts_hbm, ts_ref, load_sem.at[2])
@@ -82,34 +77,43 @@
     loads = {}
     for k in range(CHUNKS):
         for m in PAIR_ORDER:
-            col = pl.multiple_of(k * width + ((z // 2 + m) % PAIRS) * 256, 256)
+            if (k, m) == (0, PAIR_ORDER[1]):
+                barrier = pltpu.get_barrier_semaphore()
+                for d in range(1, RING):
+                    pl.semaphore_signal(barrier, inc=1, device_id=ring((z + d) & 7), device_id_type=pl.DeviceIdType.MESH)
+                for q in range(1, PLANE):
+                    pl.semaphore_signal(barrier, inc=1, device_id=plane(q), device_id_type=pl.DeviceIdType.MESH)
+                pl.semaphore_signal(barrier, inc=1, device_id=sibling, device_id_type=pl.DeviceIdType.MESH)
+            col = pl.multiple_of(k * width + (((z >> 1) + m) & 3) * 256, 256)
             loads[k, m] = pltpu.make_async_copy(
                 features.at[:, pl.ds(col, 256)], feats.at[k, m], feat_sem.at[k, m])
             loads[k, m].start()
 
+    load_t = pltpu.make_async_copy(basis, t2.at[0], load_sem.at[1])
+    load_t.start()
+    pl.semaphore_wait(barrier, RING - 1 + PLANE - 1 + 1)
+
+    near = (zl == 0) | (zl == 3)
+    edge = jnp.where(zl == 0, RING - 1, 1)
+    edge_dev = ring((z + edge) & 7)
+    inner_dev = ring((z + RING - edge) & 7)
+    my_half = pl.ds(pl.multiple_of(core * half, half), half)
+    t_out, t_on, t_sib = [], [], []
+    for i in range(PIECES):
+        piece = pl.ds(i * (n_basis // PIECES), n_basis // PIECES)
+        mine, other = basis.at[my_half, piece], t2.at[1, my_half, piece]
+        t_out.append(remote(mine, other, t_ssem.at[0, i], t_rsem.at[i], edge_dev))
+        t_on.append(remote(other, other, t_ssem.at[1, i], t_rsem.at[i], inner_dev))
+        t_sib.append(remote(other, other, u_ssem.at[i], u_rsem.at[i], sibling))
+
+    @pl.when(near)
+    def _():
+        for copy in t_out:
+            copy.start()
+
     load_ts.wait()
     load_fs.wait()
     tcol[...] = jnp.broadcast_to(ts_ref[...][None, :], (LANES, n_basis)).T
-    load_t.wait()
-    pl.semaphore_wait(barrier, RING - 1 + PLANE - 1 + 1)
-
-    near = (zl == 0) | (zl == 3)
-    edge = jnp.where(zl == 0, RING - 1, 1)
-    edge_dev = ring((z + edge) % RING)
-    inner_dev = ring((z + RING - edge) % RING)
-    my_half = pl.ds(pl.multiple_of(core * half, half), half)
-    t_out, t_on, t_sib = [], [], []
-    for i in range(2):
-        piece = pl.ds(i * mid, mid)
-        mine, other = t2.at[0, my_half, piece], t2.at[1, my_half, piece]
-        t_out.append(remote(mine, other, t_ssem.at[0, i], t_rsem.at[i], edge_dev))
-        t_on.append(remote(other, other, t_ssem.at[1, i], t_rsem.at[i], inner_dev))
-        t_sib.append(remote(other, other, u_ssem.at[i], u_rsem.at[i], sibling))
-
-    @pl.when(near)
-    def _():
-        t_out[0].start()
-        t_out[1].start()
 
     load_f.wait()
     cx, zs = {}, {}
@@ -138,40 +142,39 @@
                                zs_rsem.at[k, 0, odd], ring(in_pair(0, 1 - odd)))
             zs_recv[k, z] = (cx_own[k, 0, odd] + cx_recv[k, 0, odd]).astype(bf16)
 
-    SKEW = 3
+    def t_pass(i):
+        t_out[i].wait_recv()
+        t_on[i].start()
+        t_sib[i].start()
+
     blocks = [(k, m) for k in range(CHUNKS) for m in PAIR_ORDER]
     for i in range(len(blocks)):
         mm1(*blocks[i])
         if SKEW <= i < SKEW + PAIRS:
             pass_on(*blocks[i - SKEW])
-
-    def t_arrived(i):
-        t_out[i].wait_recv()
-        t_sib[i].start()
+        if i >= SKEW + PAIRS:
+            pl.when(near)(functools.partial(t_pass, i - SKEW - PAIRS))
 
     @pl.when(near)
     def _():
-        for i in range(2):
-            t_out[i].wait_recv()
-            t_on[i].start()
-            t_sib[i].start()
-
-    tt[0] = t2[0].T
-    for k in range(1, CHUNKS):
-        for copy in [c for (kk, *_), c in zs.items() if kk == k - 1]:
-            copy.wait_send()
-        for m in PAIR_ORDER:
-            pass_on(k, m)
+        for i in range(len(blocks) - SKEW - PAIRS, PIECES):
+            t_pass(i)
+
+    for key, copy in zs.items():
+        copy.wait_send()
+    sent = set(zs)
+    for m in PAIR_ORDER:
+        pass_on(1, m)
 
     @pl.when(jnp.logical_not(near))
     def _():
-        for i in range(2):
+        for i in range(PIECES):
             t_out[i].wait_recv()
             t_sib[i].start()
 
-    for i in range(2):
+    load_t.wait()
+    for i in range(PIECES):
         t_sib[i].wait_recv()
-    tt[1] = t2[1].T
 
     cs, ss, ms, fw = {}, {}, {}, {}
 
@@ -193,12 +196,13 @@
             swapped = swap(packed)
             low = jnp.concatenate([jnp.where(left, packed, 0), jnp.where(left, swapped, 0)], axis=0).astype(bf16)
             high = jnp.concatenate([jnp.where(left, 0, swapped), jnp.where(left, 0, packed)], axis=0).astype(bf16)
-            add = (jnp.dot(tt[g, :mid], low, preferred_element_type=f32)
-                   + jnp.dot(tt[g, mid:], high, preferred_element_type=f32))
+            contract = (((0,), (0,)), ((), ()))
+            add = (lax.dot_general(t2[g, :, :mid], low, contract, preferred_element_type=f32)
+                   + lax.dot_general(t2[g, :, mid:], high, contract, preferred_element_type=f32))
             total = add if total is None else total + add
         c_send[k] = total.astype(bf16)
         for q in PLANE_FAR_FIRST:
-            target = ((x + q // 4) % 4) * 4 + (y + q % 4) % 4
+            target = ((x + q // 4) & 3) * 4 + ((y + q % 4) & 3)
             src = c_send.at[k, pl.ds(pl.multiple_of(target * part, part), part)]
             cs[k, q] = send(src, c_recv.at[k, q], c_ssem.at[k, q], c_rsem.at[k, q], plane(q))
 
@@ -233,7 +237,7 @@
         for m in PAIR_ORDER[:-1]:
             for e in range(2):
                 dest = in_pair(m, e)
-                ms[k, m, e] = send(m_send.at[k, (dest // 4 + zh) % 2], m_all.at[k, PAIRS - m, odd, core],
+                ms[k, m, e] = send(m_send.at[k, (dest >> 2) ^ zh], m_all.at[k, PAIRS - m, odd, core],
                                    m_ssem.at[k, m, e], m_rsem.at[k, PAIRS - m, odd], ring(dest))
         ms[k, 0, 0] = send(m_send.at[k, 0], m_all.at[k, 0, odd, core],
                            m_ssem.at[k, 0, 0], m_rsem.at[k, 0, odd], ring(in_pair(0, 1 - odd)))
@@ -296,7 +300,7 @@
     for copy in t_sib:
         copy.wait_send()
     for key, copy in zs.items():
-        if key[0] == CHUNKS - 1:
+        if key not in sent:
             copy.wait_send()
     for copies in (cx, cs, ss, ms, fw):
         for copy in copies.values():
@@ -313,7 +317,7 @@
     dma = pltpu.SemaphoreType.DMA
     return pl.pallas_call(
         kernel,
-        out_shape=jax.ShapeDtypeStruct((rows, sites), bf16),
+        out_shape=pltpu.VMEM((rows, sites), bf16),
         in_specs=[any_space] * 5,
         out_specs=pl.BlockSpec(memory_space=pltpu.VMEM),
         scratch_shapes=[
@@ -323,7 +327,6 @@
             pltpu.VMEM((CHUNKS, PAIRS, 256, sites), bf16),
             pltpu.VMEM((rows, sites), bf16),
             pltpu.VMEM((2, rows, n_basis), bf16),
-            pltpu.VMEM((2, n_basis, rows), bf16),
             pltpu.VMEM((n_basis, LANES), f32),
             pltpu.VMEM((rows, sites), f32),
             pltpu.VMEM((CHUNKS, PAIRS, 2, half, LANES), f32),
@@ -338,7 +341,7 @@
             pltpu.VMEM((CHUNKS, 2, half, LANES), bf16),
             pltpu.VMEM((CHUNKS, PAIRS, 2, 2, half, LANES), bf16),
             dma((4,)), dma((CHUNKS, PAIRS)),
-            dma((2, 2)), dma((2,)), dma((2,)), dma((2,)),
+            dma((2, PIECES)), dma((PIECES,)), dma((PIECES,)), dma((PIECES,)),
             dma((CHUNKS, PAIRS)), dma((CHUNKS, PAIRS)),
             dma((CHUNKS, PAIRS, 2)), dma((CHUNKS, PAIRS, 2)),
             dma((CHUNKS, PLANE)), dma((CHUNKS, PLANE)),

time: 58.4 us -> 54.1 us (0.926)
  Pallas kernels: 56.2 us -> 53.1 us
  local copies, waits for them, and re-layouts: 2.09 us -> 0.89 us
    pallas_call x1, Pallas kernels: 56.2 us -> 53.1 us  [per_device(): pl.pallas_call(kernel, out_shape=pltpu.VMEM((rows, sites), bf16), in_spec...]
    unnamed x1, local copies, waits for them, and re-layouts: 2.09 us -> 0.89 us
where the time goes in v3:
time: 54.1 us; the launch traced here: 54 us
  Pallas kernels  53.1 us (98%)
  local copies, waits for them, and re-layouts  0.89 us (2%)
    pallas_call x1, Pallas kernels, per_device(): pl.pallas_call(kernel, out_shape=pltpu.VMEM((rows, sites), bf16), in_spec...  53.1 us

profile of v3, /device:TPU:1, one launch (start us, length us, event | category | flops | bytes accessed | tf_op | source)
XLA Modules:
  0.0 54.0 jit_solution(17847528548583338056)
XLA Ops:
  0.0 53.1 %solve.1 = bf16[160,2560]{1,0:T(8,128)(2,1)S(1)} custom-call(bf16[160,2560]{1,0:T(8,128)(2,1)} %fields.1, bf16[160,1536]{1,0:T(8,128)(2,1)} %basis.1, bf16[2560,2048]{1,0:T(8,128)(2,1)} %features.1, f32[1536]{0:T(1024)} %ts_hbm.1, f32[2048]{0:T(1024)} %fs_hbm.1), custom_call_target="tpu_custom_call" | custom-call | flops 3600000000 | bytes 13000000 | tf_op jit(solution)/shard_map/solve/pallas_call | solution.py:318
  53.1 0.9 %copy.7 = bf16[160,2560]{1,0:T(8,128)(2,1)} copy(bf16[160,2560]{1,0:T(8,128)(2,1)S(1)} %solve.1) | data formatting | bytes 1638400

commit v4 on v0

v4 whole, which is shorter than its diff:
```python
import functools

import jax
import jax.numpy as jnp
from jax import lax
from jax.experimental import pallas as pl
from jax.experimental.pallas import tpu as pltpu
from jax.sharding import PartitionSpec as P

noise_var = 0.1

RING = 8
PAIRS = 4
PLANE = 16
PIECES = 4
LANES = 128
ORDER = (2, 1, 3, 0)
LINE_ORDER = (2, 3, 1, 0)
PLANE_FAR_FIRST = (10, 6, 14, 9, 11, 2, 8, 5, 7, 13, 15, 1, 3, 4, 12)
f32 = jnp.float32
bf16 = jnp.bfloat16


def kernel(fields, basis, features, ts_hbm, fs_hbm, out,
           ts_ref, fs_ref, feats, featst, fbuf, t2, tcol, acc,
           lx_own, lx_send, lx_recv, lz_send, lz_recv, lc_send, lc_recv, lp_send, lp_recv, ls_own, ls_all, lm_send, lm_all,
           cx_own, cx_send, cx_recv, zs_send, zs_recv, c_send, c_recv, s_own, s_all, m_send, m_all,
           load_sem, feat_sem, t_ssem, t_rsem, u_ssem, u_rsem,
           lx_ssem, lx_rsem, lz_ssem, lz_rsem, lc_ssem, lc_rsem, lp_ssem, lp_rsem, ls_ssem, ls_rsem, lm_ssem, lm_rsem,
           lf_ssem, lf_rsem,
           cx_ssem, cx_rsem, zs_ssem, zs_rsem, c_ssem, c_rsem, s_ssem, s_rsem, m_ssem, m_rsem, f_ssem, f_rsem):
    hour, site = lax.axis_index("hour"), lax.axis_index("site")
    zh, x, y = hour >> 4, (hour >> 2) & 3, hour & 3
    zl, core = site >> 1, site & 1
    z = zh * 4 + zl
    odd = z & 1
    rows = fields.shape[0]
    half = rows // 2
    n_basis = basis.shape[1]
    mid = n_basis // 2
    width = features.shape[1] // 2
    part = n_basis // PLANE
    small = mid // PLANE
    left = lax.broadcasted_iota(jnp.int32, (1, LANES), 1) < LANES // 2
    contract = (((0,), (0,)), ((), ()))

    def at(z_, x_, y_, c_):
        return ((z_ >> 2) * 16 + x_ * 4 + y_, (z_ & 3) * 2 + c_)

    def ring(z_):
        return at(z_, x, y, core)

    def line(m):
        return at(z ^ m, x, y, core)

    def plane(q):
        return at(z, (x + q // 4) & 3, (y + q % 4) & 3, core)

    def plane_index(q):
        return ((x + q // 4) & 3) * 4 + ((y + q % 4) & 3)

    def in_pair(m, e):
        return (((z >> 1) + m) & 3) * 2 + e

    sibling = at(z, x, y, 1 - core)

    def remote(src, dst, ssem, rsem, device):
        return pltpu.make_async_remote_copy(
            src_ref=src, dst_ref=dst, send_sem=ssem, recv_sem=rsem,
            device_id=device, device_id_type=pl.DeviceIdType.MESH)

    def send(*args):
        copy = remote(*args)
        copy.start()
        return copy

    def swap(v):
        return pltpu.roll(v, LANES // 2, axis=1)

    load_f = pltpu.make_async_copy(fields, fbuf, load_sem.at[0])
    load_f.start()
    blocks = [("line", m) for m in LINE_ORDER] + [("ring", m) for m in ORDER]
    loads = {}
    for i, (kind, m) in enumerate(blocks):
        if kind == "line":
            col, slot = (zl ^ m) * 256, 0
        else:
            col, slot = width + (((z >> 1) + m) & 3) * 256, 1
        loads[kind, m] = pltpu.make_async_copy(
            features.at[:, pl.ds(pl.multiple_of(col, 256), 256)], feats.at[slot, m], feat_sem.at[slot, m])
        loads[kind, m].start()
        if i == 0:
            barrier = pltpu.get_barrier_semaphore()
            for d in (4, 3, 5, 2, 6, 1, 7):
                pl.semaphore_signal(barrier, inc=1, device_id=ring((z + d) & 7), device_id_type=pl.DeviceIdType.MESH)
            for q in PLANE_FAR_FIRST:
                pl.semaphore_signal(barrier, inc=1, device_id=plane(q), device_id_type=pl.DeviceIdType.MESH)
            pl.semaphore_signal(barrier, inc=1, device_id=sibling, device_id_type=pl.DeviceIdType.MESH)
    load_t = pltpu.make_async_copy(basis, t2.at[0], load_sem.at[1])
    load_t.start()
    load_ts = pltpu.make_async_copy(ts_hbm, ts_ref, load_sem.at[2])
    load_ts.start()
    load_fs = pltpu.make_async_copy(fs_hbm, fs_ref, load_sem.at[3])
    load_fs.start()
    pl.semaphore_wait(barrier, RING - 1 + PLANE - 1 + 1)

    near = (zl == 0) | (zl == 3)
    edge = jnp.where(zl == 0, RING - 1, 1)
    edge_dev = ring((z + edge) & 7)
    inner_dev = ring((z + RING - edge) & 7)
    my_half = pl.ds(pl.multiple_of(core * half, half), half)
    t_out, t_on, t_sib = [], [], []
    for i in range(PIECES):
        piece = pl.ds(i * (n_basis // PIECES), n_basis // PIECES)
        mine, other = basis.at[my_half, piece], t2.at[1, my_half, piece]
        t_out.append(remote(mine, other, t_ssem.at[0, i], t_rsem.at[i], edge_dev))
        t_on.append(remote(other, other, t_ssem.at[1, i], t_rsem.at[i], inner_dev))
        t_sib.append(remote(other, other, u_ssem.at[i], u_rsem.at[i], sibling))

    @pl.when(near)
    def _():
        for copy in t_out:
            copy.start()

    def t_pass(i):
        t_out[i].wait_recv()
        t_on[i].start()
        t_sib[i].start()

    load_f.wait()
    lx, lz, cx, zs = {}, {}, {}, {}

    def product(kind, m):
        loads[kind, m].wait()
        return jnp.dot(fbuf[...], feats[0 if kind == "line" else 1, m], preferred_element_type=f32)

    def line_product(m):
        block = product("line", m)
        low, high = block[:, :LANES], block[:, LANES:]
        lx_own[m] = jnp.where(core == 0, low, high)
        lx_send[m] = jnp.where(core == 0, high, low)
        lx[m] = send(lx_send.at[m], lx_recv.at[m], lx_ssem.at[m], lx_rsem.at[m], sibling)

    def line_pass(m):
        lx[m].wait_recv()
        if m:
            lz_send[m] = (lx_own[m] + lx_recv[m]).astype(bf16)
            lz[m] = send(lz_send.at[m], lz_recv.at[m], lz_ssem.at[m], lz_rsem.at[m], line(m))

    def ring_product(m):
        block = product("ring", m)
        for e in range(2):
            top, low = block[:half, e * LANES:(e + 1) * LANES], block[half:, e * LANES:(e + 1) * LANES]
            first = jnp.where(left, top, swap(low))
            second = jnp.where(left, swap(top), low)
            cx_own[m, e] = jnp.where(core == 0, first, second)
            cx_send[m, e] = jnp.where(core == 0, second, first)
        cx[m] = send(cx_send.at[m], cx_recv.at[m], cx_ssem.at[m], cx_rsem.at[m], sibling)

    def ring_pass(m):
        cx[m].wait_recv()
        if m:
            for e in range(2):
                zs_send[m, e] = (cx_own[m, e] + cx_recv[m, e]).astype(bf16)
                zs[m, e] = send(zs_send.at[m, e], zs_recv.at[z], zs_ssem.at[m, e],
                                zs_rsem.at[PAIRS - m, odd], ring(in_pair(m, e)))
        else:
            zs_send[0, 0] = (cx_own[0, 1 - odd] + cx_recv[0, 1 - odd]).astype(bf16)
            zs[0, 0] = send(zs_send.at[0, 0], zs_recv.at[z], zs_ssem.at[0, 0],
                            zs_rsem.at[0, odd], ring(in_pair(0, 1 - odd)))
            zs_recv[z] = (cx_own[0, odd] + cx_recv[0, odd]).astype(bf16)

    for m in LINE_ORDER[:2]:
        line_product(m)
    for i in range(2, PAIRS):
        line_product(LINE_ORDER[i])
        line_pass(LINE_ORDER[i - 2])
    for i in range(PAIRS):
        ring_product(ORDER[i])
        if i < 2:
            line_pass(LINE_ORDER[i + 2])
        else:
            pl.when(near)(functools.partial(t_pass, i - 2))

    @pl.when(near)
    def _():
        for i in range(2, PIECES):
            t_pass(i)

    for copy in lz.values():
        copy.wait_send()
    for m in ORDER:
        ring_pass(m)

    load_ts.wait()
    load_fs.wait()
    tcol[...] = jnp.broadcast_to(ts_ref[...][None, :], (LANES, n_basis)).T
    load_t.wait()

    lc, lp, ls, lm, lf = {}, {}, {}, {}, {}
    cs, ss, ms, fw = {}, {}, {}, {}
    mine_r = (x * 4 + y) * part
    own_r = pl.ds(pl.multiple_of(mine_r, part), part)
    small_r = (x * 4 + y) * small
    own_s = pl.ds(pl.multiple_of(small_r, small), small)
    own_s2 = pl.ds(pl.multiple_of(mid + small_r, small), small)

    def line_mm2():
        total = lx_own[0] + lx_recv[0]
        for m in reversed(LINE_ORDER[:-1]):
            lz[m].wait_recv()
            total = total + lz_recv[m].astype(f32)
        lc_send[...] = lax.dot_general(t2[0], total.astype(bf16), contract, preferred_element_type=f32).astype(bf16)
        for q in PLANE_FAR_FIRST:
            src = lc_send.at[pl.ds(pl.multiple_of(plane_index(q) * part, part), part)]
            lc[q] = send(src, lc_recv.at[q], lc_ssem.at[q], lc_rsem.at[q], plane(q))

    def line_trade():
        total = lc_send[own_r].astype(f32)
        for q in reversed(PLANE_FAR_FIRST):
            lc[q].wait_recv()
            total = total + lc_recv[q].astype(f32)
        lp_send[...] = total.astype(bf16)
        lp[0] = send(lp_send, lp_recv, lp_ssem.at[0], lp_rsem.at[0], ring(z ^ 4))
        return total

    def line_scale(total):
        own_f = fs_ref[pl.ds(pl.multiple_of(zl * 256 + core * LANES, LANES), LANES)][None, :]
        denom = tcol[own_r] + own_f + noise_var
        lp[0].wait_recv()
        scaled = ((total + lp_recv[...].astype(f32)) / denom).astype(bf16)
        ls_own[...] = scaled
        ls_all[own_r] = scaled
        for q in PLANE_FAR_FIRST:
            ls[q] = send(ls_own, ls_all.at[own_r], ls_ssem.at[q], ls_rsem.at[q], plane(q))

    def line_mm3():
        for q in reversed(PLANE_FAR_FIRST):
            ls[q].wait_recv()
        mixed = jnp.dot(t2[0], ls_all[...], preferred_element_type=f32).astype(bf16)
        lm_send[...] = mixed
        lm_all[0, core] = mixed
        for m in LINE_ORDER[:-1]:
            lm[m] = send(lm_send, lm_all.at[m, core], lm_ssem.at[m], lm_rsem.at[m], line(m))

    def line_forward():
        for m in reversed(LINE_ORDER):
            if m:
                lm[m].wait_recv()
            slot = lm_all.at[m, core]
            lf[m] = send(slot, slot, lf_ssem.at[m], lf_rsem.at[m], sibling)

    def line_mm4():
        total = None
        for m in reversed(LINE_ORDER):
            lf[m].wait_recv()
            block = jnp.concatenate([lm_all[m, 0], lm_all[m, 1]], axis=1)
            add = jnp.dot(block, featst[0, m], preferred_element_type=f32)
            total = add if total is None else total + add
        return total

    def wait_ring(sem, src, dst):
        for m in range(1, PAIRS):
            for e in range(2):
                remote(src, dst, sem.at[m, e], sem.at[m, e], sibling).wait_recv()
        other = sem.at[0, 1 - odd]
        remote(src, dst, other, other, sibling).wait_recv()

    def ring_mm2():
        wait_ring(zs_rsem, zs_send.at[0, 0], zs_recv.at[0])
        total = None
        for g in range(2):
            base = (zh if g == 0 else 1 - zh) * 4
            packed = ((zs_recv[base].astype(f32) + zs_recv[base + 1].astype(f32))
                      + (zs_recv[base + 2].astype(f32) + zs_recv[base + 3].astype(f32)))
            swapped = swap(packed)
            low = jnp.concatenate([jnp.where(left, packed, 0), jnp.where(left, swapped, 0)], axis=0).astype(bf16)
            high = jnp.concatenate([jnp.where(left, 0, swapped), jnp.where(left, 0, packed)], axis=0).astype(bf16)
            add = (lax.dot_general(t2[g, :, :mid], low, contract, preferred_element_type=f32)
                   + lax.dot_general(t2[g, :, mid:], high, contract, preferred_element_type=f32))
            total = add if total is None else total + add
        c_send[...] = total.astype(bf16)
        for q in PLANE_FAR_FIRST:
            src = c_send.at[pl.ds(pl.multiple_of(plane_index(q) * small, small), small)]
            cs[q] = send(src, c_recv.at[q], c_ssem.at[q], c_rsem.at[q], plane(q))

    def ring_scale():
        total = c_send[own_s].astype(f32)
        own_f = fs_ref[pl.ds(pl.multiple_of(width + z * LANES, LANES), LANES)][None, :]
        other_f = swap(jnp.broadcast_to(own_f, (8, LANES)))[:1]
        both = jnp.where(left == (core == 0), own_f, other_f)
        denom = jnp.where(left, tcol[own_s], tcol[own_s2]) + both + noise_var
        for q in reversed(PLANE_FAR_FIRST):
            cs[q].wait_recv()
            total = total + c_recv[q].astype(f32)
        scaled = (total / denom).astype(bf16)
        s_own[...] = scaled
        s_all[own_s] = scaled
        for q in PLANE_FAR_FIRST:
            ss[q] = send(s_own, s_all.at[own_s], s_ssem.at[q], s_rsem.at[q], plane(q))

    def ring_mm3():
        for q in reversed(PLANE_FAR_FIRST):
            ss[q].wait_recv()
        for g in range(2):
            first = jnp.dot(t2[g, :, :mid], s_all[...], preferred_element_type=f32)
            second = jnp.dot(t2[g, :, mid:], s_all[...], preferred_element_type=f32)
            both = jnp.where(left, first, second)
            both = both + swap(both)
            m_send[g] = jnp.where(left, both[:half], both[half:]).astype(bf16)
        for m in ORDER[:-1]:
            for e in range(2):
                dest = in_pair(m, e)
                ms[m, e] = send(m_send.at[(dest >> 2) ^ zh], m_all.at[PAIRS - m, odd, core],
                                m_ssem.at[m, e], m_rsem.at[PAIRS - m, odd], ring(dest))
        ms[0, 0] = send(m_send.at[0], m_all.at[0, odd, core],
                        m_ssem.at[0, 0], m_rsem.at[0, odd], ring(in_pair(0, 1 - odd)))
        m_all[0, odd, core] = m_send[0]

    def ring_forward():
        for m in (0, 1, 3, 2):
            for i in range(2):
                e = i ^ odd if m == 0 else i
                slot = m_all.at[m, e, core]
                if m or i:
                    sem = m_rsem.at[m, e]
                    remote(slot, slot, sem, sem, sibling).wait_recv()
                fw[m, i] = send(slot, slot, f_ssem.at[m, e], f_rsem.at[m, e], sibling)

    def ring_mm4():
        total = None
        for m in (0, 1, 3, 2):
            sides = []
            for e in range(2):
                slot = m_all.at[m, e, core]
                remote(slot, slot, f_ssem.at[m, e], f_rsem.at[m, e], sibling).wait_recv()
                first, second = m_all[m, e, 0].astype(f32), m_all[m, e, 1].astype(f32)
                sides.append(jnp.concatenate([jnp.where(left, first, swap(second)),
                                              jnp.where(left, swap(first), second)], axis=0).astype(bf16))
            block = jnp.concatenate(sides, axis=1)
            add = jnp.dot(block, featst[1, m], preferred_element_type=f32)
            total = add if total is None else total + add
        return total

    def turn(k):
        for m in range(PAIRS):
            featst[k, m] = feats[k, m].T

    line_mm2()

    @pl.when(jnp.logical_not(near))
    def _():
        for i in range(PIECES):
            t_out[i].wait_recv()
            t_sib[i].start()

    turn(0)
    line_sum = line_trade()
    for i in range(PIECES):
        t_sib[i].wait_recv()
    ring_mm2()
    line_scale(line_sum)
    turn(1)
    ring_scale()
    line_mm3()
    ring_mm3()
    line_forward()
    acc[...] = line_mm4()
    ring_forward()
    out[...] = (acc[...] + ring_mm4()).astype(out.dtype)

    @pl.when(near)
    def _():
        for copy in t_out + t_on:
            copy.wait_send()

    for copy in t_sib:
        copy.wait_send()
    for copies in (lx, lc, lp, ls, lm, lf, cx, zs, cs, ss, ms, fw):
        for copy in copies.values():
            copy.wait_send()


def per_device(fields, basis, features, time_spectrum, feature_spectrum):
    rows, sites = fields.shape
    half = rows // 2
    n_basis = basis.shape[1]
    mid = n_basis // 2
    part = n_basis // PLANE
    small = mid // PLANE
    any_space = pl.BlockSpec(memory_space=pl.ANY)
    vmem = pltpu.VMEM
    dma = pltpu.SemaphoreType.DMA
    return pl.pallas_call(
        kernel,
        out_shape=pltpu.VMEM((rows, sites), bf16),
        in_specs=[any_space] * 5,
        out_specs=pl.BlockSpec(memory_space=pltpu.VMEM),
        scratch_shapes=[
            vmem(time_spectrum.shape, f32),
            vmem(feature_spectrum.shape, f32),
            vmem((2, PAIRS, sites, 256), bf16),
            vmem((2, PAIRS, 256, sites), bf16),
            vmem((rows, sites), bf16),
            vmem((2, rows, n_basis), bf16),
            vmem((n_basis, LANES), f32),
            vmem((rows, sites), f32),
            vmem((PAIRS, rows, LANES), f32),
            vmem((PAIRS, rows, LANES), f32),
            vmem((PAIRS, rows, LANES), f32),
            vmem((PAIRS, rows, LANES), bf16),
            vmem((PAIRS, rows, LANES), bf16),
            vmem((n_basis, LANES), bf16),
            vmem((PLANE, part, LANES), bf16),
            vmem((part, LANES), bf16),
            vmem((part, LANES), bf16),
            vmem((part, LANES), bf16),
            vmem((n_basis, LANES), bf16),
            vmem((rows, LANES), bf16),
            vmem((PAIRS, 2, rows, LANES), bf16),
            vmem((PAIRS, 2, half, LANES), f32),
            vmem((PAIRS, 2, half, LANES), f32),
            vmem((PAIRS, 2, half, LANES), f32),
            vmem((PAIRS, 2, half, LANES), bf16),
            vmem((RING, half, LANES), bf16),
            vmem((mid, LANES), bf16),
            vmem((PLANE, small, LANES), bf16),
            vmem((small, LANES), bf16),
            vmem((mid, LANES), bf16),
            vmem((2, half, LANES), bf16),
            vmem((PAIRS, 2, 2, half, LANES), bf16),
            dma((4,)), dma((2, PAIRS)),
            dma((2, PIECES)), dma((PIECES,)), dma((PIECES,)), dma((PIECES,)),
            dma((PAIRS,)), dma((PAIRS,)), dma((PAIRS,)), dma((PAIRS,)),
            dma((PLANE,)), dma((PLANE,)), dma((1,)), dma((1,)), dma((PLANE,)), dma((PLANE,)),
            dma((PAIRS,)), dma((PAIRS,)), dma((PAIRS,)), dma((PAIRS,)),
            dma((PAIRS,)), dma((PAIRS,)), dma((PAIRS, 2)), dma((PAIRS, 2)),
            dma((PLANE,)), dma((PLANE,)), dma((PLANE,)), dma((PLANE,)),
            dma((PAIRS, 2)), dma((PAIRS, 2)), dma((PAIRS, 2)), dma((PAIRS, 2)),
        ],
        compiler_params=pltpu.CompilerParams(
            collective_id=0, has_side_effects=True, vmem_limit_bytes=60 * 2**20),
        cost_estimate=pl.CostEstimate(flops=3_600_000_000, bytes_accessed=13_000_000, transcendentals=0),
        name="solve",
    )(fields, basis, features, time_spectrum, feature_spectrum)


def solution(mesh):
    in_specs = (P("hour", "site"), P("hour", None), P("site", None), P(), P())
    out_specs = P("hour", "site")
    return jax.shard_map(
        per_device, mesh=mesh, in_specs=in_specs, out_specs=out_specs, check_vma=False
    )
```

time: 529 us -> 51.7 us (0.10)
  waiting for transfers between devices: 453 us -> 0 us
  Pallas kernels: 0 us -> 50.7 us
  blocking collectives: 38.9 us -> 0 us
  matrix products: 21.4 us -> 0 us
  between operations: 13.4 us -> 0.01 us
    psum x1 -> x0, waiting for transfers between devices: 410 us -> none  [per_device(): lax.psum(lax.dot_general(columns, projected, (((0,), (1,)), ((), ())), pr...]
    pallas_call x0 -> x1, Pallas kernels: none -> 50.7 us  [per_device(): pl.pallas_call(kernel, out_shape=pltpu.VMEM((rows, sites), bf16), in_spec...]
    reduce_scatter x1 -> x0, waiting for transfers between devices: 42.3 us -> none  [per_device(): lax.psum_scatter(lax.dot_general(columns, fields, (((0,), (1,)), ((), ())...]
    all_gather x1 -> x0, blocking collectives: 38.9 us -> none  [per_device(): lax.all_gather(mixed, 'site', axis=1, tiled=True)]
    dot_general x4 -> x0, matrix products: 21.4 us -> none  [the longest x1 8.69 us: per_device(): lax.dot_general(lax.all_gather(mixed, 'site', axis=1, tiled=True), column...]
  transfers between devices with their start and end apart: 2 -> 0, of which waited for: 2 -> 0; matrix products, arithmetic and copies ran while one was open for 0% -> 0% of each run, Pallas kernels for 0% -> 0%
where the time goes in v4:
time: 51.7 us; the launch traced here: 51.6 us
  Pallas kernels  50.7 us (98%)
  local copies, waits for them, and re-layouts  0.89 us (2%)
    pallas_call x1, Pallas kernels, per_device(): pl.pallas_call(kernel, out_shape=pltpu.VMEM((rows, sites), bf16), in_spec...  50.7 us

profile of v4, /device:TPU:1, one launch (start us, length us, event | category | flops | bytes accessed | tf_op | source)
XLA Modules:
  0.0 51.6 jit_solution(12699114624250624317)
XLA Ops:
  0.0 50.7 %solve.1 = bf16[160,2560]{1,0:T(8,128)(2,1)S(1)} custom-call(bf16[160,2560]{1,0:T(8,128)(2,1)} %fields.1, bf16[160,1536]{1,0:T(8,128)(2,1)} %basis.1, bf16[2560,2048]{1,0:T(8,128)(2,1)} %features.1, f32[1536]{0:T(1024)} %ts_hbm.1, f32[2048]{0:T(1024)} %fs_hbm.1), custom_call_target="tpu_custom_call" | custom-call | flops 3600000000 | bytes 13000000 | tf_op jit(solution)/shard_map/solve/pallas_call | solution.py:394
  50.7 0.9 %copy.7 = bf16[160,2560]{1,0:T(8,128)(2,1)} copy(bf16[160,2560]{1,0:T(8,128)(2,1)S(1)} %solve.1) | data formatting | bytes 1638400

commit v5 on v4

--- a/solution.py
+++ b/solution.py
@@ -102,8 +102,6 @@
     load_ts.start()
     load_fs = pltpu.make_async_copy(fs_hbm, fs_ref, load_sem.at[3])
     load_fs.start()
-    pl.semaphore_wait(barrier, RING - 1 + PLANE - 1 + 1)
-
     near = (zl == 0) | (zl == 3)
     edge = jnp.where(zl == 0, RING - 1, 1)
     edge_dev = ring((z + edge) & 7)
@@ -117,11 +115,6 @@
         t_on.append(remote(other, other, t_ssem.at[1, i], t_rsem.at[i], inner_dev))
         t_sib.append(remote(other, other, u_ssem.at[i], u_rsem.at[i], sibling))
 
-    @pl.when(near)
-    def _():
-        for copy in t_out:
-            copy.start()
-
     def t_pass(i):
         t_out[i].wait_recv()
         t_on[i].start()
@@ -139,6 +132,8 @@
         low, high = block[:, :LANES], block[:, LANES:]
         lx_own[m] = jnp.where(core == 0, low, high)
         lx_send[m] = jnp.where(core == 0, high, low)
+
+    def line_swap(m):
         lx[m] = send(lx_send.at[m], lx_recv.at[m], lx_ssem.at[m], lx_rsem.at[m], sibling)
 
     def line_pass(m):
@@ -170,17 +165,32 @@
                             zs_rsem.at[0, odd], ring(in_pair(0, 1 - odd)))
             zs_recv[z] = (cx_own[0, odd] + cx_recv[0, odd]).astype(bf16)
 
-    for m in LINE_ORDER[:2]:
+    for m in LINE_ORDER[:1]:
         line_product(m)
+    pl.semaphore_wait(barrier, RING - 1 + PLANE - 1 + 1)
+
+    @pl.when(near)
+    def _():
+        for copy in t_out:
+            copy.start()
+
+    for m in LINE_ORDER[:1]:
+        line_swap(m)
+    line_product(LINE_ORDER[1])
+    line_swap(LINE_ORDER[1])
+    line_product(LINE_ORDER[2])
+    line_swap(LINE_ORDER[2])
+    line_pass(LINE_ORDER[0])
+    line_product(LINE_ORDER[3])
+    line_swap(LINE_ORDER[3])
+    line_pass(LINE_ORDER[1])
+    ring_product(ORDER[0])
+    line_pass(LINE_ORDER[2])
+    ring_product(ORDER[1])
+    line_pass(LINE_ORDER[3])
     for i in range(2, PAIRS):
-        line_product(LINE_ORDER[i])
-        line_pass(LINE_ORDER[i - 2])
-    for i in range(PAIRS):
         ring_product(ORDER[i])
-        if i < 2:
-            line_pass(LINE_ORDER[i + 2])
-        else:
-            pl.when(near)(functools.partial(t_pass, i - 2))
+        pl.when(near)(functools.partial(t_pass, i - 2))
 
     @pl.when(near)
     def _():
@@ -243,21 +253,16 @@
         for m in LINE_ORDER[:-1]:
             lm[m] = send(lm_send, lm_all.at[m, core], lm_ssem.at[m], lm_rsem.at[m], line(m))
 
-    def line_forward():
-        for m in reversed(LINE_ORDER):
-            if m:
-                lm[m].wait_recv()
-            slot = lm_all.at[m, core]
-            lf[m] = send(slot, slot, lf_ssem.at[m], lf_rsem.at[m], sibling)
-
-    def line_mm4():
-        total = None
-        for m in reversed(LINE_ORDER):
-            lf[m].wait_recv()
-            block = jnp.concatenate([lm_all[m, 0], lm_all[m, 1]], axis=1)
-            add = jnp.dot(block, featst[0, m], preferred_element_type=f32)
-            total = add if total is None else total + add
-        return total
+    def line_forward(m):
+        if m:
+            lm[m].wait_recv()
+        slot = lm_all.at[m, core]
+        lf[m] = send(slot, slot, lf_ssem.at[m], lf_rsem.at[m], sibling)
+
+    def line_mm4(m):
+        lf[m].wait_recv()
+        block = jnp.concatenate([lm_all[m, 0], lm_all[m, 1]], axis=1)
+        return jnp.dot(block, featst[0, m], preferred_element_type=f32)
 
     def wait_ring(sem, src, dst):
         for m in range(1, PAIRS):
@@ -317,30 +322,24 @@
                         m_ssem.at[0, 0], m_rsem.at[0, odd], ring(in_pair(0, 1 - odd)))
         m_all[0, odd, core] = m_send[0]
 
-    def ring_forward():
-        for m in (0, 1, 3, 2):
-            for i in range(2):
-                e = i ^ odd if m == 0 else i
-                slot = m_all.at[m, e, core]
-                if m or i:
-                    sem = m_rsem.at[m, e]
-                    remote(slot, slot, sem, sem, sibling).wait_recv()
-                fw[m, i] = send(slot, slot, f_ssem.at[m, e], f_rsem.at[m, e], sibling)
-
-    def ring_mm4():
-        total = None
-        for m in (0, 1, 3, 2):
-            sides = []
-            for e in range(2):
-                slot = m_all.at[m, e, core]
-                remote(slot, slot, f_ssem.at[m, e], f_rsem.at[m, e], sibling).wait_recv()
-                first, second = m_all[m, e, 0].astype(f32), m_all[m, e, 1].astype(f32)
-                sides.append(jnp.concatenate([jnp.where(left, first, swap(second)),
-                                              jnp.where(left, swap(first), second)], axis=0).astype(bf16))
-            block = jnp.concatenate(sides, axis=1)
-            add = jnp.dot(block, featst[1, m], preferred_element_type=f32)
-            total = add if total is None else total + add
-        return total
+    def ring_forward(m):
+        for i in range(2):
+            e = i ^ odd if m == 0 else i
+            slot = m_all.at[m, e, core]
+            if m or i:
+                sem = m_rsem.at[m, e]
+                remote(slot, slot, sem, sem, sibling).wait_recv()
+            fw[m, i] = send(slot, slot, f_ssem.at[m, e], f_rsem.at[m, e], sibling)
+
+    def ring_mm4(m):
+        sides = []
+        for e in range(2):
+            slot = m_all.at[m, e, core]
+            remote(slot, slot, f_ssem.at[m, e], f_rsem.at[m, e], sibling).wait_recv()
+            first, second = m_all[m, e, 0].astype(f32), m_all[m, e, 1].astype(f32)
+            sides.append(jnp.concatenate([jnp.where(left, first, swap(second)),
+                                          jnp.where(left, swap(first), second)], axis=0).astype(bf16))
+        return jnp.dot(jnp.concatenate(sides, axis=1), featst[1, m], preferred_element_type=f32)
 
     def turn(k):
         for m in range(PAIRS):
@@ -364,10 +363,20 @@
     ring_scale()
     line_mm3()
     ring_mm3()
-    line_forward()
-    acc[...] = line_mm4()
-    ring_forward()
-    out[...] = (acc[...] + ring_mm4()).astype(out.dtype)
+    last = [("line", m) for m in reversed(LINE_ORDER)] + [("ring", m) for m in (0, 1, 3, 2)]
+    for i in range(len(last) + 1):
+        if i < len(last):
+            (line_forward if last[i][0] == "line" else ring_forward)(last[i][1])
+        if i == 0:
+            continue
+        kind, m = last[i - 1]
+        add = line_mm4(m) if kind == "line" else ring_mm4(m)
+        if i == 1:
+            acc[...] = add
+        elif i < len(last):
+            acc[...] += add
+        else:
+            out[...] = (acc[...] + add).astype(out.dtype)
 
     @pl.when(near)
     def _():

time: 51.7 us -> 50.9 us (0.985)
  Pallas kernels: 50.7 us -> 49.9 us
    pallas_call x1, Pallas kernels: 50.7 us -> 49.9 us  [per_device(): pl.pallas_call(kernel, out_shape=pltpu.VMEM((rows, sites), bf16), in_spec...]
where the time goes in v5:
time: 50.9 us; the launch traced here: 50.8 us
  Pallas kernels  49.9 us (98%)
  local copies, waits for them, and re-layouts  0.89 us (2%)
    pallas_call x1, Pallas kernels, per_device(): pl.pallas_call(kernel, out_shape=pltpu.VMEM((rows, sites), bf16), in_spec...  49.9 us

profile of v5, /device:TPU:1, one launch (start us, length us, event | category | flops | bytes accessed | tf_op | source)
XLA Modules:
  0.0 50.8 jit_solution(5415373562842653725)
XLA Ops:
  0.0 49.9 %solve.1 = bf16[160,2560]{1,0:T(8,128)(2,1)S(1)} custom-call(bf16[160,2560]{1,0:T(8,128)(2,1)} %fields.1, bf16[160,1536]{1,0:T(8,128)(2,1)} %basis.1, bf16[2560,2048]{1,0:T(8,128)(2,1)} %features.1, f32[1536]{0:T(1024)} %ts_hbm.1, f32[2048]{0:T(1024)} %fs_hbm.1), custom_call_target="tpu_custom_call" | custom-call | flops 3600000000 | bytes 13000000 | tf_op jit(solution)/shard_map/solve/pallas_call | solution.py:403
  49.9 0.9 %copy.7 = bf16[160,2560]{1,0:T(8,128)(2,1)} copy(bf16[160,2560]{1,0:T(8,128)(2,1)S(1)} %solve.1) | data formatting | bytes 1638400

commit v6 on v5

--- a/solution.py
+++ b/solution.py
@@ -34,6 +34,7 @@
     zl, core = site >> 1, site & 1
     z = zh * 4 + zl
     odd = z & 1
+    owner = zl ^ (3 * zh)
     rows = fields.shape[0]
     half = rows // 2
     n_basis = basis.shape[1]
@@ -83,7 +84,7 @@
     loads = {}
     for i, (kind, m) in enumerate(blocks):
         if kind == "line":
-            col, slot = (zl ^ m) * 256, 0
+            col, slot = (owner ^ m) * 256, 0
         else:
             col, slot = width + (((z >> 1) + m) & 3) * 256, 1
         loads[kind, m] = pltpu.make_async_copy(
@@ -231,11 +232,11 @@
             lc[q].wait_recv()
             total = total + lc_recv[q].astype(f32)
         lp_send[...] = total.astype(bf16)
-        lp[0] = send(lp_send, lp_recv, lp_ssem.at[0], lp_rsem.at[0], ring(z ^ 4))
+        lp[0] = send(lp_send, lp_recv, lp_ssem.at[0], lp_rsem.at[0], ring(z ^ 7))
         return total
 
     def line_scale(total):
-        own_f = fs_ref[pl.ds(pl.multiple_of(zl * 256 + core * LANES, LANES), LANES)][None, :]
+        own_f = fs_ref[pl.ds(pl.multiple_of(owner * 256 + core * LANES, LANES), LANES)][None, :]
         denom = tcol[own_r] + own_f + noise_var
         lp[0].wait_recv()
         scaled = ((total + lp_recv[...].astype(f32)) / denom).astype(bf16)
@@ -345,6 +346,11 @@
         for m in range(PAIRS):
             featst[k, m] = feats[k, m].T
 
+    def sent(*groups):
+        for copies in groups:
+            for copy in copies.values():
+                copy.wait_send()
+
     line_mm2()
 
     @pl.when(jnp.logical_not(near))
@@ -354,21 +360,39 @@
             t_sib[i].start()
 
     turn(0)
+    sent(lx, cx)
     line_sum = line_trade()
     for i in range(PIECES):
         t_sib[i].wait_recv()
     ring_mm2()
+    sent(lc)
     line_scale(line_sum)
     turn(1)
+    sent(zs, lp)
     ring_scale()
+    sent(cs)
+
+    @pl.when(near)
+    def _():
+        for copy in t_out + t_on:
+            copy.wait_send()
+
+    for copy in t_sib:
+        copy.wait_send()
     line_mm3()
+    sent(ls)
     ring_mm3()
+    sent(ss)
     last = [("line", m) for m in reversed(LINE_ORDER)] + [("ring", m) for m in (0, 1, 3, 2)]
     for i in range(len(last) + 1):
         if i < len(last):
             (line_forward if last[i][0] == "line" else ring_forward)(last[i][1])
         if i == 0:
             continue
+        if i == PAIRS + 1:
+            sent(lm)
+        if i == len(last):
+            sent(lf, ms)
         kind, m = last[i - 1]
         add = line_mm4(m) if kind == "line" else ring_mm4(m)
         if i == 1:
@@ -377,17 +401,7 @@
             acc[...] += add
         else:
             out[...] = (acc[...] + add).astype(out.dtype)
-
-    @pl.when(near)
-    def _():
-        for copy in t_out + t_on:
-            copy.wait_send()
-
-    for copy in t_sib:
-        copy.wait_send()
-    for copies in (lx, lc, lp, ls, lm, lf, cx, zs, cs, ss, ms, fw):
-        for copy in copies.values():
-            copy.wait_send()
+    sent(fw)
 
 
 def per_device(fields, basis, features, time_spectrum, feature_spectrum):

time: 50.9 us -> 50.7 us (level)
  no operation moved by 1% of the time
where the time goes in v6:
time: 50.7 us
  Pallas kernels  49.8 us (98%)
  local copies, waits for them, and re-layouts  0.89 us (2%)
    pallas_call x1, Pallas kernels, per_device(): pl.pallas_call(kernel, out_shape=pltpu.VMEM((rows, sites), bf16), in_spec...  49.8 us

profile of v6, /device:TPU:1, one launch (start us, length us, event | category | flops | bytes accessed | tf_op | source)
XLA Modules:
  0.0 50.7 jit_solution(17031589968213082349)
XLA Ops:
  0.0 49.8 %solve.1 = bf16[160,2560]{1,0:T(8,128)(2,1)S(1)} custom-call(bf16[160,2560]{1,0:T(8,128)(2,1)} %fields.1, bf16[160,1536]{1,0:T(8,128)(2,1)} %basis.1, bf16[2560,2048]{1,0:T(8,128)(2,1)} %features.1, f32[1536]{0:T(1024)} %ts_hbm.1, f32[2048]{0:T(1024)} %fs_hbm.1), custom_call_target="tpu_custom_call" | custom-call | flops 3600000000 | bytes 13000000 | tf_op jit(solution)/shard_map/solve/pallas_call | solution.py:417
  49.8 0.9 %copy.7 = bf16[160,2560]{1,0:T(8,128)(2,1)} copy(bf16[160,2560]{1,0:T(8,128)(2,1)S(1)} %solve.1) | data formatting | bytes 1638400
